TPU v7x, 32 devices: a whole 2x2x4 slice. The times are simulated.
32 devices in a mesh: src: 4 (over y, x), tgt: 4 (over z), rep: 2 (over core).
Axes of the slice: x: 2, y: 2, z: 4, core: 2. Of those that a mesh axis runs over, the one named last changes fastest.
Arguments:
- omega: bfloat16 [128, 32768], P('rep', 'src'), may hold values from -6 to 6
- leaf: bfloat16 [4, 64, 32768], P('tgt', None, 'src'), may hold values from -0.0625 to 0.0625
- factors: bfloat16 [4, 4, 2, 64, 128], P('tgt', 'src'), may hold values from -0.5 to 0.5
- pattern: int32 [4, 4, 2, 2, 4], P('tgt', 'src'), may hold values 0 or 1
- ranks: int32 [2], replicated, may hold values from 32 to 64
- outer: bfloat16 [64, 8192], P(None, ('tgt', 'src')), may hold values from -0.375 to 0.375
Outputs:
- samples: float32 [128, 8192], P('rep', ('tgt', 'src'))
All inputs are finite; a program needn't handle non-finite values. No bound on the sum of `pattern` on one device may be relied on, other than what follows from the above.
Results may differ from a plain program's by a relative error of at most 0.02.
Values may be sent and summed in bfloat16 or wider, within the bound.
A program may use at most 64 MiB of HBM per device.

v0:
```python
import jax
import jax.numpy as jnp
from jax import lax
from jax.sharding import PartitionSpec as P

K = 64
R_ALL = 128
BLK = 32
LEVELS = 2
NS_ITERS = 3


def partner_2(block, axis, apart):
    count = lax.axis_size(axis)
    route = []
    for low in range(count):
        high = low | 1 << apart
        if high != low and high < count:
            route += [(low, high), (high, low)]
    return lax.ppermute(block, axis, route)


def contract_leading(left, right):
    return lax.dot_general(
        left, right, (((0,), (0,)), ((), ())), preferred_element_type=jnp.float32
    )


def contract_trailing(left, right):
    return lax.dot_general(
        left, right, (((1,), (1,)), ((), ())), preferred_element_type=jnp.float32
    )


def whiten(gram, fresh):
    scale = jnp.sqrt(jnp.sum(gram * gram)) + 1e-06
    upper = gram / scale
    eye = jnp.eye(K, dtype=jnp.float32)
    lower = eye
    for step in range(NS_ITERS):
        central_factor = 1.5 * eye - 0.5 * jnp.dot(lower, upper, precision=lax.Precision.HIGHEST)
        upper = jnp.dot(upper, central_factor, precision=lax.Precision.HIGHEST)
        lower = jnp.dot(central_factor, lower, precision=lax.Precision.HIGHEST)
    result = jnp.dot(lower, fresh.astype(jnp.float32), precision=lax.Precision.HIGHEST)
    return result * jnp.sqrt(R_ALL / scale)


def shards(omega, leaf, factors, pattern, ranks, outer):
    piece = contract_trailing(leaf[0], omega).astype(jnp.bfloat16)
    source = lax.axis_index("src")
    rows = jnp.arange(K)
    for level in range(LEVELS):
        partner = partner_2(piece, "src", level)
        lowside = source >> level & 1 == 0
        stacked = jnp.where(
            lowside, jnp.concatenate([piece, partner], 0), jnp.concatenate([partner, piece], 0)
        )
        blocks = jnp.repeat(jnp.repeat(pattern[0, 0, level], BLK, 0), BLK, 1)
        masked = factors[0, 0, level] * blocks.astype(jnp.bfloat16)
        fresh = jnp.dot(masked, stacked, preferred_element_type=jnp.float32).astype(jnp.bfloat16)
        gram = lax.psum(contract_trailing(fresh, fresh), "rep")
        whitened = whiten(gram, fresh)
        piece = jnp.where((rows < ranks[level])[:, None], whitened, 0.0).astype(jnp.bfloat16)
    block_bases = lax.all_gather(outer, "src", axis=1, tiled=True)
    mine = lax.psum_scatter(
        contract_leading(block_bases, piece).astype(jnp.bfloat16),
        "src",
        scatter_dimension=0,
        tiled=True,
    ).astype(jnp.float32)
    return mine.T


def solution(mesh):
    return jax.shard_map(
        shards,
        mesh=mesh,
        in_specs=(
            P("rep", "src"),
            P("tgt", None, "src"),
            P("tgt", "src", None, None, None),
            P("tgt", "src", None, None, None),
            P(),
            P(None, ("tgt", "src")),
        ),
        out_specs=P("rep", ("tgt", "src")),
        check_vma=False,
    )
```

profile of v0, /device:TPU:0, one launch (start us, length us, event | category | flops | bytes accessed | tf_op | source)
XLA Modules:
  0.0 72.7 jit_solution(14658556601859107056)
XLA Ops:
  6.5 1.2 %copy-done = bf16[64,8192]{1,0:T(8,128)(2,1)S(1)} copy-done((bf16[64,8192]{1,0:T(8,128)(2,1)S(1)}, bf16[64,8192]{1,0:T(8,128)(2,1)}, u32[]{:S(2)}) %copy-start) | copy-done | bytes 1048600
  7.8 1.6 %convolution_convert_fusion.3 = bf16[64,64]{0,1:T(8,128)(2,1)S(1)} fusion(bf16[64,8192]{1,0:T(8,128)(2,1)S(1)} %copy-done, bf16[1,64,8192]{2,1,0:T(8,128)(2,1)} %param.7), kind=kOutput, calls=%fused_computation.22 | convolution fusion | flops 67112960 | bytes 2105344 | tf_op jit(solution)/shard_map/dot_general | solution.py:30
  9.4 3.0 %collective-permute-start = (bf16[64,64]{0,1:T(8,128)(2,1)S(1)}, bf16[64,64]{0,1:T(8,128)(2,1)S(1)}, u32[]{:S(2)}, u32[]{:S(2)}) collective-permute-start(bf16[64,64]{0,1:T(8,128)(2,1)S(1)} %convolution_convert_fusion.3), channel_id=1, source_target_pairs={{0,8},{8,0},{16,24},{24,16},{1,9},{9,1},{17,25},{25,17},{2,10},{10... | collective-permute-start | bytes 24584 | tf_op jit(solution)/shard_map/ppermute | solution.py:20
  12.4 0.6 copy-done.4
  13.1 0.6 fusion.31
  13.7 0.6 iota_compare_fusion.6
  14.4 0.7 iota_compare_fusion.5
  15.1 0.1 copy.11
  15.2 0.1 broadcast_in_dim.34
  15.2 0.1 convert_element_type.54
  15.3 0.1 copy.15
  15.5 0.2 convolution_convert_fusion.2
  15.7 0.1 fusion.32
  15.8 3.4 %psum.14 = f32[64,64]{1,0:T(8,128)S(1)} all-reduce(f32[64,64]{1,0:T(8,128)S(1)} %fusion.32), channel_id=1, replica_groups=mesh['src'=4,'tgt'=4,'rep'=2] {'rep'}, use_global_device_ids=true, to_apply=%region_0.1 | all-reduce | flops 4096 | bytes 32768 | tf_op jit(solution)/shard_map/psum | solution.py:61
  19.2 0.6 multiply_reduce_fusion.1
  20.5 0.2 fusion.8
  20.7 0.2 fusion.26
  20.9 0.1 fusion.18
  21.0 0.2 fusion.7
  21.2 0.2 fusion.33
  21.4 0.2 fusion.34
  21.6 0.2 fusion.6
  21.8 0.0 copy-start.1
  21.8 0.2 fusion.35
  22.0 0.1 fusion.9
  22.1 1.6 %collective-permute-start.1 = (bf16[64,64]{1,0:T(8,128)(2,1)S(1)}, bf16[64,64]{1,0:T(8,128)(2,1)S(1)}, u32[]{:S(2)}, u32[]{:S(2)}) collective-permute-start(bf16[64,64]{1,0:T(8,128)(2,1)S(1)} %fusion.9), channel_id=1, source_target_pairs={{0,16},{16,0},{8,24},{24,8},{1,17},{17,1},{9,25},{25,9},{2,18},{18... | collective-permute-start | bytes 24584 | tf_op jit(solution)/shard_map/ppermute | solution.py:20
  23.7 8.1 %all_gather.3 = bf16[64,2048]{1,0:T(8,128)(2,1)S(1)} all-gather(bf16[64,512]{1,0:T(8,128)(2,1)S(1)} %copy-done.1), channel_id=1, replica_groups=mesh['src'=4,'tgt'=4,'rep'=2] {'src'}, dimensions={1}, use_global_device_ids=true | all-gather | bytes 327680 | tf_op jit(solution)/shard_map/all_gather | solution.py:64
  31.9 0.1 copy.9
  32.0 0.1 broadcast_in_dim.31
  32.0 0.1 convert_element_type.51
  32.1 0.1 copy.14
  32.3 0.2 convolution_convert_fusion.1
  32.5 0.1 fusion.36
  32.6 3.4 %psum.15 = f32[64,64]{1,0:T(8,128)S(1)} all-reduce(f32[64,64]{1,0:T(8,128)S(1)} %fusion.36), channel_id=1, replica_groups=mesh['src'=4,'tgt'=4,'rep'=2] {'rep'}, use_global_device_ids=true, to_apply=%region_2.3 | all-reduce | flops 4096 | bytes 32768 | tf_op jit(solution)/shard_map/psum | solution.py:61
  36.0 0.6 multiply_reduce_fusion
  37.3 0.2 fusion.4
  37.5 0.2 fusion.27
  37.7 0.1 fusion.17
  37.8 0.2 fusion.3
  38.0 0.2 fusion.37
  38.2 0.2 fusion.38
  38.4 0.2 fusion.2
  38.6 0.2 fusion.39
  38.7 0.1 fusion.10
  38.9 1.0 %fusion = bf16[2048,64]{0,1:T(8,128)(2,1)} fusion(bf16[64,64]{1,0:T(8,128)(2,1)S(1)} %fusion.10, bf16[64,2048]{1,0:T(8,128)(2,1)S(1)} %all_gather.3), kind=kOutput, calls=%fused_computation.1 | convolution fusion | flops 16908288 | bytes 532480 | tf_op jit(solution)/shard_map/dot_general | solution.py:24
  39.8 0.0 reduce-scatter.2.cloned.1.call-update
  39.9 24.5 %reduce-scatter.2.cloned.1.call-done = bf16[512,64]{0,1:T(8,128)(2,1)} async-done(((bf16[2048,64]{0,1:T(8,128)(2,1)}), bf16[512,64]{0,1:T(8,128)(2,1)}) %reduce-scatter.2.cloned.1.call-update) | async-done | bytes 65552 | tf_op jit(solution)/shard_map/reduce_scatter | solution.py:65
  64.4 1.5 %convert_bitcast_fusion = f32[64,512]{1,0:T(8,128)} fusion(bf16[512,64]{0,1:T(8,128)(2,1)} %reduce-scatter.2.cloned.1.call-done), kind=kLoop, calls=%fused_computation.24 | loop fusion | flops 32768 | bytes 196608 | tf_op jit(solution)/shard_map/transpose | solution.py:71
  (15 shorter events, 0.1 us)
Async XLA Ops:
  6.5 1.2 %copy-start = (bf16[64,8192]{1,0:T(8,128)(2,1)S(1)}, bf16[64,8192]{1,0:T(8,128)(2,1)}, u32[]{:S(2)}) copy-start(bf16[64,8192]{1,0:T(8,128)(2,1)} %param.6) | copy-start | bytes 3145732
  6.5 5.9 %copy-start.3 = (s32[1,1,2,2,4]{4,3,2,1,0:T(2,128)S(1)}, s32[1,1,2,2,4]{4,3,2,1,0:T(2,128)}, u32[]{:S(2)}) copy-start(s32[1,1,2,2,4]{4,3,2,1,0:T(2,128)} %param.9) | copy-start | bytes 196
  6.5 57.8 %reduce-scatter.2.cloned.1.call-start = ((), (), s32[]{:S(2)}) async-start(), calls=%async_computation.1 | async-start | bytes 327680 | tf_op jit(solution)/shard_map/reduce_scatter | solution.py:65
  7.8 6.6 %copy-start.2 = (bf16[1,1,2,64,128]{4,3,2,1,0:T(8,128)(2,1)S(1)}, bf16[1,1,2,64,128]{4,3,2,1,0:T(8,128)(2,1)}, u32[]{:S(2)}) copy-start(bf16[1,1,2,64,128]{4,3,2,1,0:T(8,128)(2,1)} %param.8) | copy-start | bytes 98308
  9.4 6.1 %collective-permute-start = (bf16[64,64]{0,1:T(8,128)(2,1)S(1)}, bf16[64,64]{0,1:T(8,128)(2,1)S(1)}, u32[]{:S(2)}, u32[]{:S(2)}) collective-permute-start(bf16[64,64]{0,1:T(8,128)(2,1)S(1)} %convolution_convert_fusion.3), channel_id=1, source_target_pairs={{0,8},{8,0},{16,24},{24,16},{1,9},{9,1},{17,25},{25,17},{2,10},{10... | collective-permute-start | bytes 24584 | tf_op jit(solution)/shard_map/ppermute | solution.py:20
  12.4 0.7 copy-start.4
  21.8 1.9 %copy-start.1 = (bf16[64,512]{1,0:T(8,128)(2,1)S(1)}, bf16[64,512]{1,0:T(8,128)(2,1)}, u32[]{:S(2)}) copy-start(bf16[64,512]{1,0:T(8,128)(2,1)} %param.11) | copy-start | bytes 196612
  22.1 10.1 %collective-permute-start.1 = (bf16[64,64]{1,0:T(8,128)(2,1)S(1)}, bf16[64,64]{1,0:T(8,128)(2,1)S(1)}, u32[]{:S(2)}, u32[]{:S(2)}) collective-permute-start(bf16[64,64]{1,0:T(8,128)(2,1)S(1)} %fusion.9), channel_id=1, source_target_pairs={{0,16},{16,0},{8,24},{24,8},{1,17},{17,1},{9,25},{25,9},{2,18},{18... | collective-permute-start | bytes 24584 | tf_op jit(solution)/shard_map/ppermute | solution.py:20
Sparse Core Ops, SparseCore 0:
  40.0 24.3 reduce-scatter.1
where the time goes:
time: 73 us; the launch traced here: 72.7 us
  waiting for transfers between devices  24.5 us (34%)
  between operations  15.2 us (21%)
  blocking collectives  15 us (21%)
  matrix products  6.11 us (8%)
  starting transfers between devices  4.59 us (6%)
  other arithmetic  4.08 us (6%)
  local copies, waits for them, and re-layouts  3.24 us (4%)
    reduce_scatter x1, waiting for transfers between devices, shards(): lax.psum_scatter(contract_leading(block_bases, piece).astype(jnp.bfloat16...  24.5 us
    all_gather x1, blocking collectives, shards(): block_bases = lax.all_gather(outer, 'src', axis=1, tiled=True)  8.15 us
    psum x2, blocking collectives, shards(): gram = lax.psum(contract_trailing(fresh, fresh), 'rep')  6.82 us
    ppermute x2, starting transfers between devices, partner_2(): return lax.ppermute(block, axis, route)  4.59 us
    unnamed x12, local copies, waits for them, and re-layouts  2.1 us
    dot_general x3, matrix products, contract_trailing(): lax.dot_general(left, right, (((1,), (1,)), ((), ())), preferred_element_...  1.9 us
    transpose x1, other arithmetic, shards(): return mine.T  1.5 us
  transfers between devices with their start and end apart: 3, of which 1 were waited for; matrix products, arithmetic and copies ran while one was open for 4% of the time, Pallas kernels for 0%

commit v1 on v0

v1 whole, which is shorter than its diff:
```python
import jax
import jax.numpy as jnp
from jax import lax
from jax.experimental import pallas as pl
from jax.experimental.pallas import tpu as pltpu
from jax.sharding import PartitionSpec as P

K = 64
R_ALL = 128
BLK = 32
LEVELS = 2
GROUP = 4
CHUNKS = 4
MESH = pl.DeviceIdType.MESH

F32 = jnp.float32
BF16 = jnp.bfloat16


def product(left, right, dims=((1,), (0,))):
    return lax.dot_general(
        left.astype(BF16), right.astype(BF16), (dims, ((), ())), preferred_element_type=F32
    )


def level_slot(level, source):
    if level == 0:
        return source
    return source // 2 + 2 * (source % 2)


def whiten(fresh_bf, own):
    eye = (
        lax.broadcasted_iota(jnp.int32, (K, K), 0) == lax.broadcasted_iota(jnp.int32, (K, K), 1)
    ).astype(F32)
    count = len(fresh_bf)
    each = range(count)
    gram = [product(f, f, ((1,), (1,))) for f in fresh_bf]
    squared = [product(g, g) for g in gram]
    norm = [jnp.sum(jnp.sum(g * g, axis=1, keepdims=True), axis=0, keepdims=True) for g in gram]
    scale = [jnp.sqrt(n) + 1e-06 for n in norm]
    inv = [1.0 / s for s in scale]
    gain = [jnp.sqrt(R_ALL * i) for i in inv]
    a = [g * i for g, i in zip(gram, inv)]
    t = [s * i * i for s, i in zip(squared, inv)]
    target = [f[:, :K] if own else f for f in fresh_bf]
    w = [1.5 * target[i].astype(F32) - 0.5 * product(a[i], target[i]) for i in each]
    p = [2.25 * a[i] - 1.5 * t[i] + 0.25 * product(t[i], a[i]) for i in each]
    q = [product(p[i], p[i]) for i in each]
    w = [1.5 * w[i] - 0.5 * product(p[i], w[i]) for i in each]
    p = [2.25 * p[i] - 1.5 * q[i] + 0.25 * product(q[i], p[i]) for i in each]
    w = [1.5 * w[i] - 0.5 * product(p[i], w[i]) for i in each]
    return [w[i] * gain[i] for i in each]


def kernel(
    omega_hbm, leaf_hbm, factors_hbm, pattern_hbm, ranks_hbm, outer_hbm, out_ref,
    omega, leaf, factors, pattern, ranks, outer, masked, gathered,
    load_sem, chunk_sem, fsend, frecv, psend, precv, *, finish,
):
    src = lax.axis_index("src")
    tgt = lax.axis_index("tgt")
    rep = lax.axis_index("rep")
    base = src - lax.rem(src, GROUP)
    me = src - base

    def peer(step, other):
        return (base + lax.rem(me + step, GROUP), tgt, lax.rem(rep + other, 2))

    peers = [(step, other) for other in (0, 1) for step in range(GROUP) if (step, other) != (0, 0)]
    barrier = pltpu.get_barrier_semaphore()
    for step, other in peers:
        pl.semaphore_signal(barrier, inc=1, device_id=peer(step, other), device_id_type=MESH)

    small = [
        pltpu.make_async_copy(a, b, load_sem.at[i])
        for i, (a, b) in enumerate(
            (
                (pattern_hbm, pattern),
                (factors_hbm.at[0, 0], factors),
                (ranks_hbm, ranks),
            )
        )
    ]
    load_outer = pltpu.make_async_copy(outer_hbm, outer, load_sem.at[3])
    for copy in small:
        copy.start()
    width = omega.shape[1] // CHUNKS
    big = []
    for c in range(CHUNKS):
        cols = pl.ds(c * width, width)
        pair = (
            pltpu.make_async_copy(omega_hbm.at[:, cols], omega.at[:, cols], chunk_sem.at[0, c]),
            pltpu.make_async_copy(leaf_hbm.at[0, :, cols], leaf.at[:, cols], chunk_sem.at[1, c]),
        )
        for copy in pair:
            copy.start()
        big.append(pair)
    load_outer.start()

    for copy in small:
        copy.wait()
    lane = lax.broadcasted_iota(jnp.int32, (1, 2 * K), 1) // BLK
    for level in range(LEVELS):
        at = pl.multiple_of(level_slot(level, me) * K, K)
        for i in range(K // BLK):
            keep = jnp.zeros((1, 2 * K), F32)
            for j in range(2 * K // BLK):
                keep = jnp.where(lane == j, pattern[0, 0, level, i, j].astype(F32), keep)
            block = factors[level, i * BLK:(i + 1) * BLK, :].astype(F32) * keep
            masked[level, pl.ds(at + i * BLK, BLK), :] = block.astype(BF16)

    pl.semaphore_wait(barrier, len(peers))
    fcopies = []
    for level in range(LEVELS):
        at = pl.multiple_of(level_slot(level, me) * K, K)
        rows = masked.at[level, pl.ds(at, K), :]
        for step in range(1, GROUP):
            copy = pltpu.make_async_remote_copy(
                src_ref=rows, dst_ref=rows,
                send_sem=fsend.at[level, step], recv_sem=frecv.at[level, step],
                device_id=peer(step, 0), device_id_type=MESH,
            )
            copy.start()
            fcopies.append(copy)

    piece = jnp.zeros((K, K), F32)
    for c in range(CHUNKS):
        for copy in big[c]:
            copy.wait()
        cols = slice(c * width, (c + 1) * width)
        piece = piece + product(leaf[:, cols], omega[:, cols], ((1,), (1,)))
    at = pl.multiple_of(me * K, K)
    gathered[0, pl.ds(at, K), :] = piece.astype(BF16)
    pcopies = []
    for step, other in peers:
        copy = pltpu.make_async_remote_copy(
            src_ref=gathered.at[0, pl.ds(at, K), :],
            dst_ref=gathered.at[other, pl.ds(at, K), :],
            send_sem=psend.at[other, step], recv_sem=precv.at[other, step],
            device_id=peer(step, other), device_id_type=MESH,
        )
        copy.start()
        pcopies.append(copy)

    for copy in fcopies:
        copy.wait_recv()
    for copy in pcopies:
        copy.wait_recv()

    row = lax.broadcasted_iota(jnp.int32, (K, 1), 0)
    stacks = [
        jnp.concatenate([gathered[0, h * 2 * K:(h + 1) * 2 * K, :],
                         gathered[1, h * 2 * K:(h + 1) * 2 * K, :]], axis=1)
        for h in range(2)
    ]
    order = (0, 1, 2, 3)
    for level in range(LEVELS):
        fresh = []
        for h in range(2):
            both = product(masked[level, h * 2 * K:(h + 1) * 2 * K, :], stacks[h]).astype(BF16)
            fresh += [both[:K], both[K:]]
        pieces = whiten(fresh, level == LEVELS - 1)
        pieces = [jnp.where(row < ranks[level], x, 0.0).astype(BF16) for x in pieces]
        if level == 0:
            stacks = [
                jnp.concatenate([pieces[0], pieces[2]], axis=0),
                jnp.concatenate([pieces[1], pieces[3]], axis=0),
            ]
    total = (pieces[0].astype(F32) + pieces[1].astype(F32)) + (
        pieces[2].astype(F32) + pieces[3].astype(F32)
    )
    load_outer.wait()
    if finish:
        out_ref[...] = product(total, outer[...], ((0,), (0,)))
    else:
        out_ref[...] = total
    for copy in fcopies:
        copy.wait_send()
    for copy in pcopies:
        copy.wait_send()


def shards(omega, leaf, factors, pattern, ranks, outer):
    groups = lax.axis_size("src") // GROUP
    finish = groups == 1
    shape = (K, outer.shape[1]) if finish else (K, K)
    hbm = pl.BlockSpec(memory_space=pl.ANY)
    result = pl.pallas_call(
        lambda *refs: kernel(*refs, finish=finish),
        out_shape=jax.ShapeDtypeStruct(shape, F32),
        in_specs=[hbm] * 6,
        out_specs=pl.BlockSpec(memory_space=pltpu.VMEM),
        scratch_shapes=[
            pltpu.VMEM(omega.shape, BF16),
            pltpu.VMEM(leaf.shape[1:], BF16),
            pltpu.VMEM((LEVELS, K, 2 * K), BF16),
            pltpu.SMEM(pattern.shape, jnp.int32),
            pltpu.SMEM((LEVELS,), jnp.int32),
            pltpu.VMEM(outer.shape, BF16),
            pltpu.VMEM((LEVELS, GROUP * K, 2 * K), BF16),
            pltpu.VMEM((2, GROUP * K, K), BF16),
            pltpu.SemaphoreType.DMA((4,)),
            pltpu.SemaphoreType.DMA((2, CHUNKS)),
            pltpu.SemaphoreType.DMA((LEVELS, GROUP)),
            pltpu.SemaphoreType.DMA((LEVELS, GROUP)),
            pltpu.SemaphoreType.DMA((2, GROUP)),
            pltpu.SemaphoreType.DMA((2, GROUP)),
        ],
        compiler_params=pltpu.CompilerParams(
            collective_id=0, has_side_effects=True, vmem_limit_bytes=32 * 1024 * 1024
        ),
        cost_estimate=pl.CostEstimate(
            flops=2 * K * K * omega.shape[1], bytes_accessed=2 * omega.size * 2, transcendentals=0
        ),
    )(omega, leaf, factors, pattern, ranks, outer)
    if finish:
        return result
    total = lax.psum(result, "src") * (1.0 / GROUP)
    return lax.dot_general(
        total, outer.astype(F32), (((0,), (0,)), ((), ())), precision=lax.Precision.HIGHEST
    )


def solution(mesh):
    return jax.shard_map(
        shards,
        mesh=mesh,
        in_specs=(
            P("rep", "src"),
            P("tgt", None, "src"),
            P("tgt", "src", None, None, None),
            P("tgt", "src", None, None, None),
            P(),
            P(None, ("tgt", "src")),
        ),
        out_specs=P("rep", ("tgt", "src")),
        check_vma=False,
    )
```

time: 73 us -> 16.9 us (0.23)
  waiting for transfers between devices: 24.5 us -> 0 us
  between operations: 15.2 us -> 0.02 us
  blocking collectives: 15 us -> 0 us
  Pallas kernels: 0 us -> 10.5 us
  matrix products: 6.11 us -> 0 us
  starting transfers between devices: 4.59 us -> 0 us
  other arithmetic: 4.08 us -> 0 us
  local copies, waits for them, and re-layouts: 3.24 us -> 6.04 us
    reduce_scatter x1 -> x0, waiting for transfers between devices: 24.5 us -> none  [shards(): lax.psum_scatter(contract_leading(block_bases, piece).astype(jnp.bfloat16...]
    pallas_call x0 -> x1, Pallas kernels: none -> 10.5 us  [shards(): pl.pallas_call(lambda *refs: kernel(*refs, finish=finish), out_shape=jax....]
    all_gather x1 -> x0, blocking collectives: 8.15 us -> none  [shards(): block_bases = lax.all_gather(outer, 'src', axis=1, tiled=True)]
    psum x2 -> x0, blocking collectives: 6.82 us -> none  [shards(): gram = lax.psum(contract_trailing(fresh, fresh), 'rep')]
    dot_general x24 -> x0, matrix products: 6.11 us -> none  [the longest x3 1.9 us: contract_trailing(): lax.dot_general(left, right, (((1,), (1,)), ((), ())), preferred_element_...]
    ppermute x2 -> x0, starting transfers between devices: 4.59 us -> none  [partner_2(): return lax.ppermute(block, axis, route)]
    unnamed x12 -> x13, local copies, waits for them, and re-layouts: 2.1 us -> 6.04 us
    transpose x1 -> x0, other arithmetic: 1.5 us -> none  [shards(): return mine.T]
  transfers between devices with their start and end apart: 3 -> 0, of which waited for: 1 -> 0; matrix products, arithmetic and copies ran while one was open for 4% -> 0% of each run, Pallas kernels for 0% -> 0%
where the time goes in v1:
time: 16.9 us; the launch traced here: 16.5 us
  Pallas kernels  10.5 us (62%)
  local copies, waits for them, and re-layouts  6.04 us (36%)
    pallas_call x1, Pallas kernels, shards(): pl.pallas_call(lambda *refs: kernel(*refs, finish=finish), out_shape=jax....  10.5 us
    unnamed x13, local copies, waits for them, and re-layouts  6.04 us

profile of v1, /device:TPU:0, one launch (start us, length us, event | category | flops | bytes accessed | tf_op | source)
XLA Modules:
  0.0 16.5 jit_solution(3028855356427111833)
XLA Ops:
  0.0 0.0 copy-start
  0.0 1.2 %copy-done = bf16[64,8192]{1,0:T(8,128)(2,1)S(1)} copy-done((bf16[64,8192]{1,0:T(8,128)(2,1)S(1)}, bf16[64,8192]{1,0:T(8,128)(2,1)}, u32[]{:S(2)}) %copy-start) | copy-done | bytes 1048600
  1.2 0.0 copy-start.1
  1.2 1.2 %copy-done.1 = bf16[1,64,8192]{2,1,0:T(8,128)(2,1)S(1)} copy-done((bf16[1,64,8192]{2,1,0:T(8,128)(2,1)S(1)}, bf16[1,64,8192]{2,1,0:T(8,128)(2,1)}, u32[]{:S(2)}) %copy-start.1) | copy-done | bytes 1048600
  2.5 0.0 copy-start.2
  2.5 0.8 %copy-done.2 = bf16[64,512]{1,0:T(8,128)(2,1)S(1)} copy-done((bf16[64,512]{1,0:T(8,128)(2,1)S(1)}, bf16[64,512]{1,0:T(8,128)(2,1)}, u32[]{:S(2)}) %copy-start.2) | copy-done | bytes 65560
  3.3 0.0 copy-start.3
  3.3 0.8 %copy-done.3 = bf16[1,1,2,64,128]{4,3,2,1,0:T(8,128)(2,1)S(1)} copy-done((bf16[1,1,2,64,128]{4,3,2,1,0:T(8,128)(2,1)S(1)}, bf16[1,1,2,64,128]{4,3,2,1,0:T(8,128)(2,1)}, u32[]{:S(2)}) %copy-start.3) | copy-done | bytes 32792
  4.0 0.0 copy-start.4
  4.1 0.7 %copy-done.4 = s32[1,1,2,2,4]{4,3,2,1,0:T(2,128)S(1)} copy-done((s32[1,1,2,2,4]{4,3,2,1,0:T(2,128)S(1)}, s32[1,1,2,2,4]{4,3,2,1,0:T(2,128)}, u32[]{:S(2)}) %copy-start.4) | copy-done | bytes 88
  4.7 0.0 copy-start.5
  4.7 0.7 %copy-done.5 = s32[2]{0:T(128)S(1)} copy-done((s32[2]{0:T(128)S(1)}, s32[2]{0:T(128)}, u32[]{:S(2)}) %copy-start.5) | copy-done | bytes 32
  5.4 10.5 %shard_map.64 = f32[64,512]{1,0:T(8,128)S(1)} custom-call(bf16[64,8192]{1,0:T(8,128)(2,1)S(1)} %copy-done, bf16[1,64,8192]{2,1,0:T(8,128)(2,1)S(1)} %copy-done.1, bf16[1,1,2,64,128]{4,3,2,1,0:T(8,128)(2,1)S(1)} %copy-done.3, s32[1,1,2,2,4]{4,3,2,1,0:T(2,128)S(1)} %copy-done.4, s32[2]{0:T(128)S(1)} %copy-done.5, bf16[64,512]{1,0:T(8,128)(2,1)S(1)} %copy-done.2), custom_call_target="tpu_custom_call" | custom-call | flops 67108864 | bytes 2097152 | tf_op jit(solution)/shard_map/pallas_call | solution.py:189
  15.9 0.7 %copy.8 = f32[64,512]{1,0:T(8,128)} copy(f32[64,512]{1,0:T(8,128)S(1)} %shard_map.64) | data formatting | bytes 262144
Async XLA Ops:
  0.0 1.2 %copy-start = (bf16[64,8192]{1,0:T(8,128)(2,1)S(1)}, bf16[64,8192]{1,0:T(8,128)(2,1)}, u32[]{:S(2)}) copy-start(bf16[64,8192]{1,0:T(8,128)(2,1)} %refs_0_.1) | copy-start | bytes 3145732
  1.2 1.2 %copy-start.1 = (bf16[1,64,8192]{2,1,0:T(8,128)(2,1)S(1)}, bf16[1,64,8192]{2,1,0:T(8,128)(2,1)}, u32[]{:S(2)}) copy-start(bf16[1,64,8192]{2,1,0:T(8,128)(2,1)} %refs_1_.1) | copy-start | bytes 3145732
  2.5 0.8 %copy-start.2 = (bf16[64,512]{1,0:T(8,128)(2,1)S(1)}, bf16[64,512]{1,0:T(8,128)(2,1)}, u32[]{:S(2)}) copy-start(bf16[64,512]{1,0:T(8,128)(2,1)} %refs_5_.1) | copy-start | bytes 196612
  3.3 0.8 %copy-start.3 = (bf16[1,1,2,64,128]{4,3,2,1,0:T(8,128)(2,1)S(1)}, bf16[1,1,2,64,128]{4,3,2,1,0:T(8,128)(2,1)}, u32[]{:S(2)}) copy-start(bf16[1,1,2,64,128]{4,3,2,1,0:T(8,128)(2,1)} %refs_2_.1) | copy-start | bytes 98308
  4.0 0.7 %copy-start.4 = (s32[1,1,2,2,4]{4,3,2,1,0:T(2,128)S(1)}, s32[1,1,2,2,4]{4,3,2,1,0:T(2,128)}, u32[]{:S(2)}) copy-start(s32[1,1,2,2,4]{4,3,2,1,0:T(2,128)} %refs_3_.1) | copy-start | bytes 196
  4.7 0.7 %copy-start.5 = (s32[2]{0:T(128)S(1)}, s32[2]{0:T(128)}, u32[]{:S(2)}) copy-start(s32[2]{0:T(128)} %refs_4_.1) | copy-start | bytes 28

commit v2 on v1

--- a/solution.py
+++ b/solution.py
@@ -65,9 +65,11 @@
     me = src - base
 
     def peer(step, other):
-        return (base + lax.rem(me + step, GROUP), tgt, lax.rem(rep + other, 2))
-
-    peers = [(step, other) for other in (0, 1) for step in range(GROUP) if (step, other) != (0, 0)]
+        high = lax.rem(me // 2 + step // 2, 2)
+        low = lax.rem(lax.rem(me, 2) + step % 2, 2)
+        return (base + 2 * high + low, tgt, lax.rem(rep + other, 2))
+
+    peers = [(3, 0), (3, 1), (1, 0), (2, 0), (1, 1), (2, 1), (0, 1)]
     barrier = pltpu.get_barrier_semaphore()
     for step, other in peers:
         pl.semaphore_signal(barrier, inc=1, device_id=peer(step, other), device_id_type=MESH)
@@ -110,52 +112,57 @@
             block = factors[level, i * BLK:(i + 1) * BLK, :].astype(F32) * keep
             masked[level, pl.ds(at + i * BLK, BLK), :] = block.astype(BF16)
 
+    piece = jnp.zeros((K, K), F32)
+    for c in range(CHUNKS):
+        for copy in big[c]:
+            copy.wait()
+        cols = slice(c * width, (c + 1) * width)
+        piece = piece + product(leaf[:, cols], omega[:, cols], ((1,), (1,)))
+    half = K // 2
+    at = pl.multiple_of(me * half, half)
+    piece = piece.astype(BF16)
+    gathered[0, pl.ds(at, half), :] = jnp.concatenate([piece[:half], piece[half:]], axis=1)
     pl.semaphore_wait(barrier, len(peers))
-    fcopies = []
+    pcopies = []
+    for step, other in peers:
+        copy = pltpu.make_async_remote_copy(
+            src_ref=gathered.at[0, pl.ds(at, half), :],
+            dst_ref=gathered.at[other, pl.ds(at, half), :],
+            send_sem=psend.at[other, step], recv_sem=precv.at[other, step],
+            device_id=peer(step, other), device_id_type=MESH,
+        )
+        copy.start()
+        pcopies.append(copy)
+    fcopies = [[], []]
     for level in range(LEVELS):
         at = pl.multiple_of(level_slot(level, me) * K, K)
         rows = masked.at[level, pl.ds(at, K), :]
-        for step in range(1, GROUP):
+        for step in (3, 1, 2):
             copy = pltpu.make_async_remote_copy(
                 src_ref=rows, dst_ref=rows,
                 send_sem=fsend.at[level, step], recv_sem=frecv.at[level, step],
                 device_id=peer(step, 0), device_id_type=MESH,
             )
             copy.start()
-            fcopies.append(copy)
-
-    piece = jnp.zeros((K, K), F32)
-    for c in range(CHUNKS):
-        for copy in big[c]:
-            copy.wait()
-        cols = slice(c * width, (c + 1) * width)
-        piece = piece + product(leaf[:, cols], omega[:, cols], ((1,), (1,)))
-    at = pl.multiple_of(me * K, K)
-    gathered[0, pl.ds(at, K), :] = piece.astype(BF16)
-    pcopies = []
-    for step, other in peers:
-        copy = pltpu.make_async_remote_copy(
-            src_ref=gathered.at[0, pl.ds(at, K), :],
-            dst_ref=gathered.at[other, pl.ds(at, K), :],
-            send_sem=psend.at[other, step], recv_sem=precv.at[other, step],
-            device_id=peer(step, other), device_id_type=MESH,
-        )
-        copy.start()
-        pcopies.append(copy)
-
-    for copy in fcopies:
-        copy.wait_recv()
+            fcopies[level].append(copy)
+
     for copy in pcopies:
         copy.wait_recv()
 
     row = lax.broadcasted_iota(jnp.int32, (K, 1), 0)
-    stacks = [
-        jnp.concatenate([gathered[0, h * 2 * K:(h + 1) * 2 * K, :],
-                         gathered[1, h * 2 * K:(h + 1) * 2 * K, :]], axis=1)
-        for h in range(2)
-    ]
-    order = (0, 1, 2, 3)
+    stacks = []
+    for h in range(2):
+        blocks = []
+        for source in (2 * h, 2 * h + 1):
+            mine, theirs = (gathered[o, source * half:(source + 1) * half, :] for o in (0, 1))
+            blocks += [
+                jnp.concatenate([mine[:, :K], theirs[:, :K]], axis=1),
+                jnp.concatenate([mine[:, K:], theirs[:, K:]], axis=1),
+            ]
+        stacks.append(jnp.concatenate(blocks, axis=0))
     for level in range(LEVELS):
+        for copy in fcopies[level]:
+            copy.wait_recv()
         fresh = []
         for h in range(2):
             both = product(masked[level, h * 2 * K:(h + 1) * 2 * K, :], stacks[h]).astype(BF16)
@@ -175,7 +182,7 @@
         out_ref[...] = product(total, outer[...], ((0,), (0,)))
     else:
         out_ref[...] = total
-    for copy in fcopies:
+    for copy in fcopies[0] + fcopies[1]:
         copy.wait_send()
     for copy in pcopies:
         copy.wait_send()
@@ -199,7 +206,7 @@
             pltpu.SMEM((LEVELS,), jnp.int32),
             pltpu.VMEM(outer.shape, BF16),
             pltpu.VMEM((LEVELS, GROUP * K, 2 * K), BF16),
-            pltpu.VMEM((2, GROUP * K, K), BF16),
+            pltpu.VMEM((2, GROUP * K // 2, 2 * K), BF16),
             pltpu.SemaphoreType.DMA((4,)),
             pltpu.SemaphoreType.DMA((2, CHUNKS)),
             pltpu.SemaphoreType.DMA((LEVELS, GROUP)),
@@ -208,7 +215,7 @@
             pltpu.SemaphoreType.DMA((2, GROUP)),
         ],
         compiler_params=pltpu.CompilerParams(
-            collective_id=0, has_side_effects=True, vmem_limit_bytes=32 * 1024 * 1024
+            collective_id=0, has_side_effects=True
         ),
         cost_estimate=pl.CostEstimate(
             flops=2 * K * K * omega.shape[1], bytes_accessed=2 * omega.size * 2, transcendentals=0

time: 16.9 us -> 13 us (0.77); the launches traced: 16.5 us -> 12.9 us
  local copies, waits for them, and re-layouts: 6.04 us -> 1.57 us
  Pallas kernels: 10.5 us -> 11.3 us
    unnamed x13 -> x1, local copies, waits for them, and re-layouts: 6.04 us -> 1.57 us
    pallas_call x1, Pallas kernels: 10.5 us -> 11.3 us  [shards(): pl.pallas_call(lambda *refs: kernel(*refs, finish=finish), out_shape=jax....]
where the time goes in v2:
time: 13 us; the launch traced here: 12.9 us
  Pallas kernels  11.3 us (87%)
  local copies, waits for them, and re-layouts  1.57 us (12%)
    pallas_call x1, Pallas kernels, shards(): pl.pallas_call(lambda *refs: kernel(*refs, finish=finish), out_shape=jax....  11.3 us
    unnamed x1, local copies, waits for them, and re-layouts  1.57 us

profile of v2, /device:TPU:0, one launch (start us, length us, event | category | flops | bytes accessed | tf_op | source)
XLA Modules:
  0.0 12.9 jit_solution(17898886993454046393)
XLA Ops:
  0.0 11.3 %shard_map.64 = f32[64,512]{1,0:T(8,128)} custom-call(bf16[64,8192]{1,0:T(8,128)(2,1)} %refs_0_.1, bf16[1,64,8192]{2,1,0:T(8,128)(2,1)} %refs_1_.1, bf16[1,1,2,64,128]{4,3,2,1,0:T(8,128)(2,1)} %refs_2_.1, s32[1,1,2,2,4]{4,3,2,1,0:T(2,128)} %refs_3_.1, s32[2]{0:T(128)} %refs_4_.1, bf16[64,512]{1,0:T(8,128)(2,1)} %refs_5_.1), custom_call_target="tpu_custom_call" | custom-call | flops 67108864 | bytes 2097152 | tf_op jit(solution)/shard_map/pallas_call | solution.py:196
  11.3 1.6 %copy.8 = f32[64,512]{1,0:T(8,128)} copy(f32[64,512]{1,0:T(8,128)} %shard_map.64) | data formatting | bytes 262144

commit v3 on v2

--- a/solution.py
+++ b/solution.py
@@ -215,12 +215,13 @@
             pltpu.SemaphoreType.DMA((2, GROUP)),
         ],
         compiler_params=pltpu.CompilerParams(
-            collective_id=0, has_side_effects=True
+            collective_id=0, has_side_effects=True, vmem_limit_bytes=32 * 1024 * 1024
         ),
         cost_estimate=pl.CostEstimate(
             flops=2 * K * K * omega.shape[1], bytes_accessed=2 * omega.size * 2, transcendentals=0
         ),
-    )(omega, leaf, factors, pattern, ranks, outer)
+    )(*(pltpu.with_memory_space_constraint(x, pltpu.HBM)
+        for x in (omega, leaf, factors, pattern, ranks, outer)))
     if finish:
         return result
     total = lax.psum(result, "src") * (1.0 / GROUP)

time: 13 us -> 11.5 us (0.88)
  local copies, waits for them, and re-layouts: 1.57 us -> 0.66 us
  Pallas kernels: 11.3 us -> 10.7 us
    unnamed x1, local copies, waits for them, and re-layouts: 1.57 us -> 0.66 us
    pallas_call x1, Pallas kernels: 11.3 us -> 10.7 us  [shards(): pl.pallas_call(lambda *refs: kernel(*refs, finish=finish), out_shape=jax....]
where the time goes in v3:
time: 11.5 us; the launch traced here: 11.3 us
  Pallas kernels  10.7 us (93%)
  local copies, waits for them, and re-layouts  0.66 us (6%)
    pallas_call x1, Pallas kernels, shards(): pl.pallas_call(lambda *refs: kernel(*refs, finish=finish), out_shape=jax....  10.7 us
    unnamed x1, local copies, waits for them, and re-layouts  0.66 us

profile of v3, /device:TPU:0, one launch (start us, length us, event | category | flops | bytes accessed | tf_op | source)
XLA Modules:
  0.0 11.3 jit_solution(4975987664639533790)
XLA Ops:
  0.0 10.7 %shard_map.64 = f32[64,512]{1,0:T(8,128)S(1)} custom-call(bf16[64,8192]{1,0:T(8,128)(2,1)} %refs_0_.1, bf16[1,64,8192]{2,1,0:T(8,128)(2,1)} %refs_1_.1, bf16[1,1,2,64,128]{4,3,2,1,0:T(8,128)(2,1)} %refs_2_.1, s32[1,1,2,2,4]{4,3,2,1,0:T(2,128)} %refs_3_.1, s32[2]{0:T(128)} %refs_4_.1, bf16[64,512]{1,0:T(8,128)(2,1)} %refs_5_.1), custom_call_target="tpu_custom_call" | custom-call | flops 67108864 | bytes 2097152 | tf_op jit(solution)/shard_map/pallas_call | solution.py:196
  10.7 0.7 %copy.8 = f32[64,512]{1,0:T(8,128)} copy(f32[64,512]{1,0:T(8,128)S(1)} %shard_map.64) | data formatting | bytes 262144

commit v4 on v3

--- a/solution.py
+++ b/solution.py
@@ -124,7 +124,9 @@
     gathered[0, pl.ds(at, half), :] = jnp.concatenate([piece[:half], piece[half:]], axis=1)
     pl.semaphore_wait(barrier, len(peers))
     pcopies = []
-    for step, other in peers:
+    fcopies = [[], []]
+
+    def send_piece(step, other):
         copy = pltpu.make_async_remote_copy(
             src_ref=gathered.at[0, pl.ds(at, half), :],
             dst_ref=gathered.at[other, pl.ds(at, half), :],
@@ -133,19 +135,24 @@
         )
         copy.start()
         pcopies.append(copy)
-    fcopies = [[], []]
-    for level in range(LEVELS):
-        at = pl.multiple_of(level_slot(level, me) * K, K)
-        rows = masked.at[level, pl.ds(at, K), :]
-        for step in (3, 1, 2):
-            copy = pltpu.make_async_remote_copy(
-                src_ref=rows, dst_ref=rows,
-                send_sem=fsend.at[level, step], recv_sem=frecv.at[level, step],
-                device_id=peer(step, 0), device_id_type=MESH,
-            )
-            copy.start()
-            fcopies[level].append(copy)
-
+
+    def send_factor(step, level):
+        rows = masked.at[level, pl.ds(pl.multiple_of(level_slot(level, me) * K, K), K), :]
+        copy = pltpu.make_async_remote_copy(
+            src_ref=rows, dst_ref=rows,
+            send_sem=fsend.at[level, step], recv_sem=frecv.at[level, step],
+            device_id=peer(step, 0), device_id_type=MESH,
+        )
+        copy.start()
+        fcopies[level].append(copy)
+
+    for step in (3, 1, 2):
+        send_factor(step, 0)
+        send_piece(step, 0)
+        send_piece(step, 1)
+    send_piece(0, 1)
+    for step in (3, 1, 2):
+        send_factor(step, 1)
     for copy in pcopies:
         copy.wait_recv()
 

time: 11.5 us -> 11.3 us (0.983)
  Pallas kernels: 10.7 us -> 10.5 us
    pallas_call x1, Pallas kernels: 10.7 us -> 10.5 us  [shards(): pl.pallas_call(lambda *refs: kernel(*refs, finish=finish), out_shape=jax....]
where the time goes in v4:
time: 11.3 us; the launch traced here: 11.2 us
  Pallas kernels  10.5 us (93%)
  local copies, waits for them, and re-layouts  0.66 us (6%)
    pallas_call x1, Pallas kernels, shards(): pl.pallas_call(lambda *refs: kernel(*refs, finish=finish), out_shape=jax....  10.5 us
    unnamed x1, local copies, waits for them, and re-layouts  0.66 us

profile of v4, /device:TPU:0, one launch (start us, length us, event | category | flops | bytes accessed | tf_op | source)
XLA Modules:
  0.0 11.2 jit_solution(8594205222081678247)
XLA Ops:
  0.0 10.5 %shard_map.64 = f32[64,512]{1,0:T(8,128)S(1)} custom-call(bf16[64,8192]{1,0:T(8,128)(2,1)} %refs_0_.1, bf16[1,64,8192]{2,1,0:T(8,128)(2,1)} %refs_1_.1, bf16[1,1,2,64,128]{4,3,2,1,0:T(8,128)(2,1)} %refs_2_.1, s32[1,1,2,2,4]{4,3,2,1,0:T(2,128)} %refs_3_.1, s32[2]{0:T(128)} %refs_4_.1, bf16[64,512]{1,0:T(8,128)(2,1)} %refs_5_.1), custom_call_target="tpu_custom_call" | custom-call | flops 67108864 | bytes 2097152 | tf_op jit(solution)/shard_map/pallas_call | solution.py:203
  10.5 0.7 %copy.8 = f32[64,512]{1,0:T(8,128)} copy(f32[64,512]{1,0:T(8,128)S(1)} %shard_map.64) | data formatting | bytes 262144
